TPU v7x, 128 devices: a whole 4x4x4 slice. The times are simulated.
128 devices in a mesh: pipe: 2 (over z_lo), dp: 32 (over x, y, core), tensor: 2 (over z_hi).
Axes of the slice: x: 4, y: 4, z: 4 (z_hi: 2, z_lo: 2; z = z_hi * 2 + z_lo), core: 2. Of those that a mesh axis runs over, the one named last changes fastest.
Arguments:
- tokens: bfloat16 [64, 256, 768], P('dp', 'tensor'), may hold values from -6 to 6
- cotangent: bfloat16 [64, 256, 768], P('dp', 'tensor'), may hold values from -6 to 6
- routes: int32 [2, 64, 256, 1], P('pipe', 'dp', 'tensor'), may hold values from 0 to 3; in each aligned block of 256 rows (0 to 255, 256 to 511, ..., all dimensions but the last counted through in order) at most 88 rows name the same one
- g_attn: bfloat16 [2, 768], P('pipe', 'dp'), may hold values from 0.099609375 to 1.8984375
- w_qkv: bfloat16 [2, 768, 3, 768], P('pipe', 'dp', None, 'tensor'), may hold values from -0.21875 to 0.21875
- w_out: bfloat16 [2, 768, 768], P('pipe', 'dp', 'tensor'), may hold values from -1.75 to 1.75
- g_moe: bfloat16 [2, 768], P('pipe', 'dp'), may hold values from 0.099609375 to 1.8984375
- w_router: bfloat16 [2, 768, 4], P('pipe', 'dp'), may hold values from -0.15625 to 0.15625
- w_in: bfloat16 [2, 4, 768, 3072], P('pipe', None, 'dp', 'tensor'), may hold values from -0.21875 to 0.21875
- w_down: bfloat16 [2, 4, 768, 3072], P('pipe', None, 'dp', 'tensor'), may hold values from -0.4375 to 0.4375
Outputs:
- hidden_states: bfloat16 [2, 64, 256, 768], P('pipe', 'dp', 'tensor')
- grad_inputs: float32 [2, 64, 256, 768], P('pipe', 'dp', 'tensor')
- grad_g_attn: float32 [2, 768], P('pipe', 'dp')
- grad_w_qkv: float32 [2, 768, 3, 768], P('pipe', 'dp', None, 'tensor')
- grad_w_out: float32 [2, 768, 768], P('pipe', 'dp', 'tensor')
- grad_g_moe: float32 [2, 768], P('pipe', 'dp')
- grad_w_router: float32 [2, 768, 4], P('pipe', 'dp')
- grad_w_in: float32 [2, 4, 768, 3072], P('pipe', None, 'dp', 'tensor')
- grad_w_down: float32 [2, 4, 768, 3072], P('pipe', None, 'dp', 'tensor')
Inputs may be any that keep to these rules, and one draw needn't show every extreme that they name: `routes`: within the 256 tokens of one sequence of a layer no expert is named more than 88 times; in some sequences one expert is named exactly 88 times.
All inputs are finite; a program needn't handle non-finite values.
Results may differ from a plain program's by a relative error of at most 0.033.
Values may be sent and summed in bfloat16 or wider, within the bound.
No kernel may reach another device: no remote copies, remote signals or barrier semaphores. Data moves between devices by JAX's collectives and lax.ppermute only.
A program may use at most 256 MiB of HBM per device.

v0:
```python
import math

import jax
import jax.numpy as jnp
from jax import lax
from jax.sharding import PartitionSpec as P

DH = 64
E = 4
CAP = 88


norm_eps = 1e-06
highest = lax.Precision.HIGHEST


def shifted_2(array, axis, by):
    size = lax.axis_size(axis)
    pairs = [(i, i + by) for i in range(size) if 0 <= i + by < size]
    return lax.ppermute(array, axis, pairs)


def rms_scale(values):
    return lax.rsqrt(jnp.mean(values * values, axis=-1, keepdims=True) + norm_eps)


def norm_back(grad_normed, values, scale_rows, gain):
    normal = values * scale_rows
    weighted = grad_normed * gain
    grad_values = scale_rows * (
        weighted - normal * jnp.mean(weighted * normal, axis=-1, keepdims=True)
    )
    return (grad_values, jnp.sum(grad_normed * normal, axis=0))


def softmax_rows(scores):
    shifted = scores - jnp.max(scores, axis=-1, keepdims=True)
    exponent = jnp.exp(shifted)
    return exponent / jnp.sum(exponent, axis=-1, keepdims=True)


def gelu_exact(values):
    return jax.nn.gelu(values, approximate=False)


def expert_onehot(route_ids):
    return route_ids[:, None] == jnp.arange(E, dtype=jnp.int32)[None, :]


def slot_index(route_ids):
    onehot = expert_onehot(route_ids).astype(jnp.int32)
    before = jnp.cumsum(onehot, axis=0) - onehot
    return (route_ids * CAP + jnp.sum(before * onehot, axis=1)).astype(jnp.int32)


def dispatch_table(slot_ids):
    return (slot_ids[None, :] == jnp.arange(E * CAP, dtype=jnp.int32)[:, None]).astype(jnp.bfloat16)


def forward(inputs, route_ids, weights):
    g_attn, w_qkv, w_out, g_moe, w_router, w_in, w_down = weights
    row_count, model_width = inputs.shape
    local_width = w_qkv.shape[2]
    head_count = local_width // DH
    score_scale = 1.0 / math.sqrt(DH)
    normed = (inputs * rms_scale(inputs) * g_attn.astype(jnp.float32)).astype(jnp.bfloat16)
    gathered = lax.all_gather(normed, "tensor", axis=0, tiled=True)
    length = gathered.shape[0]
    packed = jnp.dot(
        gathered, w_qkv.reshape(model_width, 3 * local_width), preferred_element_type=jnp.float32
    )
    query_rows = packed[:, :local_width].astype(jnp.bfloat16).reshape(length, head_count, DH)
    key_rows = (
        packed[:, local_width : 2 * local_width]
        .astype(jnp.bfloat16)
        .reshape(length, head_count, DH)
    )
    value_rows = packed[:, 2 * local_width :].astype(jnp.bfloat16).reshape(length, head_count, DH)
    scores = (
        jnp.einsum("qhd,khd->hqk", query_rows, key_rows, preferred_element_type=jnp.float32)
        * score_scale
    )
    highest_score = jnp.max(scores, axis=-1, keepdims=True)
    exponent = jnp.exp(scores - highest_score)
    exp_total = jnp.sum(exponent, axis=-1, keepdims=True)
    attn_probs = exponent / exp_total
    log_total = highest_score + jnp.log(exp_total)
    context = jnp.einsum(
        "hqk,khd->qhd",
        attn_probs.astype(jnp.bfloat16),
        value_rows,
        preferred_element_type=jnp.float32,
    )
    context = context.astype(jnp.bfloat16).reshape(length, local_width)
    projected = lax.psum_scatter(
        lax.dot_general(
            context, w_out, (((1,), (1,)), ((), ())), preferred_element_type=jnp.float32
        ),
        "tensor",
        scatter_dimension=0,
        tiled=True,
    )
    middle = inputs + projected
    mixed_rows = (middle * rms_scale(middle) * g_moe.astype(jnp.float32)).astype(jnp.bfloat16)
    router_probs = softmax_rows(jnp.dot(mixed_rows, w_router, preferred_element_type=jnp.float32))
    gate_prob = jnp.sum(jnp.where(expert_onehot(route_ids), router_probs, 0.0), axis=-1)
    mixed_all, routes_all = (
        lax.all_gather(mixed_rows, "tensor", axis=0, tiled=True),
        lax.all_gather(route_ids, "tensor", axis=0, tiled=True),
    )
    slot_ids = slot_index(routes_all)
    filled = jnp.dot(dispatch_table(slot_ids), mixed_all, preferred_element_type=jnp.float32)
    filled = filled.astype(jnp.bfloat16).reshape(E, CAP, model_width)
    hidden = jnp.einsum("ecd,edf->ecf", filled, w_in, preferred_element_type=jnp.float32)
    activated = gelu_exact(hidden).astype(jnp.bfloat16)
    expert_out = jnp.einsum(
        "ecf,edf->ecd", activated, w_down, preferred_element_type=jnp.float32
    ).reshape(E * CAP, model_width)
    combined = lax.psum_scatter(
        jnp.take(expert_out, slot_ids, axis=0).astype(jnp.bfloat16),
        "tensor",
        scatter_dimension=0,
        tiled=True,
    ).astype(jnp.float32)
    output = middle + gate_prob[:, None] * combined
    kept_values = (
        inputs,
        gathered,
        query_rows,
        key_rows,
        value_rows,
        log_total,
        context,
        middle,
        mixed_rows,
        route_ids,
        router_probs,
        gate_prob,
        combined,
        filled,
        hidden,
        slot_ids,
    )
    return (output, kept_values)


def backward(grad_out, kept_values, weights):
    (
        inputs,
        gathered,
        query_rows,
        key_rows,
        value_rows,
        log_total,
        context,
        middle,
        mixed_rows,
        route_ids,
        router_probs,
        gate_prob,
        combined,
        filled,
        hidden,
        slot_ids,
    ) = kept_values
    g_attn, w_qkv, w_out, g_moe, w_router, w_in, w_down = weights
    row_count, model_width = inputs.shape
    length, local_width = context.shape
    head_count = local_width // DH
    score_scale = 1.0 / math.sqrt(DH)
    grad_gate = jnp.sum(grad_out * combined, axis=-1)
    grad_branch = (gate_prob[:, None] * grad_out).astype(jnp.bfloat16)
    branch_rows = lax.all_gather(grad_branch, "tensor", axis=0, tiled=True)
    grad_slots = jnp.dot(dispatch_table(slot_ids), branch_rows, preferred_element_type=jnp.float32)
    grad_slots = grad_slots.astype(jnp.bfloat16).reshape(E, CAP, model_width)
    activated, gelu_pull = jax.vjp(gelu_exact, hidden)
    grad_act = jnp.einsum("ecd,edf->ecf", grad_slots, w_down, preferred_element_type=jnp.float32)
    grad_w_down = jnp.einsum(
        "ecd,ecf->edf",
        grad_slots,
        activated.astype(jnp.bfloat16),
        preferred_element_type=jnp.float32,
    )
    grad_hidden = gelu_pull(grad_act)[0].astype(jnp.bfloat16)
    grad_w_in = jnp.einsum("ecd,ecf->edf", filled, grad_hidden, preferred_element_type=jnp.float32)
    grad_filled = jnp.einsum(
        "ecf,edf->ecd", grad_hidden, w_in, preferred_element_type=jnp.float32
    ).reshape(E * CAP, model_width)
    grad_mixed = lax.psum_scatter(
        jnp.take(grad_filled, slot_ids, axis=0).astype(jnp.bfloat16),
        "tensor",
        scatter_dimension=0,
        tiled=True,
    ).astype(jnp.float32)
    grad_choice = jnp.where(expert_onehot(route_ids), grad_gate[:, None], 0.0)
    grad_logits = router_probs * (
        grad_choice - jnp.sum(grad_choice * router_probs, axis=-1, keepdims=True)
    )
    grad_w_router = jnp.dot(mixed_rows.astype(jnp.float32).T, grad_logits, precision=highest)
    grad_mixed = grad_mixed + jnp.dot(
        grad_logits, w_router.astype(jnp.float32).T, precision=highest
    )
    grad_norm_moe, grad_g_moe = norm_back(
        grad_mixed, middle, rms_scale(middle), g_moe.astype(jnp.float32)
    )
    grad_middle = grad_out + grad_norm_moe
    proj_rows = lax.all_gather(grad_middle.astype(jnp.bfloat16), "tensor", axis=0, tiled=True)
    grad_context = jnp.dot(proj_rows, w_out, preferred_element_type=jnp.float32).astype(
        jnp.bfloat16
    )
    grad_w_out = lax.dot_general(
        proj_rows, context, (((0,), (0,)), ((), ())), preferred_element_type=jnp.float32
    )
    scores = (
        jnp.einsum("qhd,khd->hqk", query_rows, key_rows, preferred_element_type=jnp.float32)
        * score_scale
    )
    attn_probs = jnp.exp(scores - log_total)
    grad_heads = grad_context.reshape(length, head_count, DH)
    grad_values = jnp.einsum(
        "hqk,qhd->khd",
        attn_probs.astype(jnp.bfloat16),
        grad_heads,
        preferred_element_type=jnp.float32,
    ).astype(jnp.bfloat16)
    grad_weights = jnp.einsum(
        "qhd,khd->hqk", grad_heads, value_rows, preferred_element_type=jnp.float32
    )
    grad_scores = attn_probs * (
        grad_weights - jnp.sum(grad_weights * attn_probs, axis=-1, keepdims=True)
    )
    grad_scores = grad_scores.astype(jnp.bfloat16)
    grad_query = (
        jnp.einsum("hqk,khd->qhd", grad_scores, key_rows, preferred_element_type=jnp.float32)
        * score_scale
    ).astype(jnp.bfloat16)
    grad_keys = (
        jnp.einsum("hqk,qhd->khd", grad_scores, query_rows, preferred_element_type=jnp.float32)
        * score_scale
    ).astype(jnp.bfloat16)
    grad_packed = jnp.concatenate(
        [
            grad_query.reshape(length, local_width),
            grad_keys.reshape(length, local_width),
            grad_values.reshape(length, local_width),
        ],
        axis=1,
    )
    grad_w_qkv = lax.dot_general(
        gathered, grad_packed, (((0,), (0,)), ((), ())), preferred_element_type=jnp.float32
    ).reshape(model_width, 3, local_width)
    packed_weight = w_qkv.reshape(model_width, 3 * local_width)
    grad_normed = lax.psum_scatter(
        lax.dot_general(
            grad_packed, packed_weight, (((1,), (1,)), ((), ())), preferred_element_type=jnp.float32
        ).astype(jnp.bfloat16),
        "tensor",
        scatter_dimension=0,
        tiled=True,
    ).astype(jnp.float32)
    grad_norm_attn, grad_g_attn = norm_back(
        grad_normed, inputs, rms_scale(inputs), g_attn.astype(jnp.float32)
    )
    grad_inputs = grad_middle + grad_norm_attn
    return (
        grad_inputs,
        (grad_g_attn, grad_w_qkv, grad_w_out, grad_g_moe, grad_w_router, grad_w_in, grad_w_down),
    )


def on_device(tokens, cotangent, routes, g_attn, w_qkv, w_out, g_moe, w_router, w_in, w_down):
    section_index = lax.axis_index("pipe")
    first_section = section_index == 0
    micro_count, row_count, model_width = tokens.shape
    route_table = routes[0, :, :, 0]
    weights = (
        lax.all_gather(g_attn[0], "dp", axis=0, tiled=True),
        lax.all_gather(w_qkv[0], "dp", axis=0, tiled=True),
        lax.all_gather(w_out[0], "dp", axis=0, tiled=True),
        lax.all_gather(g_moe[0], "dp", axis=0, tiled=True),
        lax.all_gather(w_router[0], "dp", axis=0, tiled=True),
        lax.all_gather(w_in[0], "dp", axis=1, tiled=True),
        lax.all_gather(w_down[0], "dp", axis=1, tiled=True),
    )

    def forward_tick(tick_index, received):
        micro_index = jnp.clip(tick_index - section_index, 0, micro_count - 1)
        own_rows = lax.dynamic_index_in_dim(tokens, micro_index, 0, keepdims=False).astype(
            jnp.float32
        )
        inputs = jnp.where(first_section, own_rows, received.astype(jnp.float32))
        route_ids = lax.dynamic_index_in_dim(route_table, micro_index, 0, keepdims=False)
        output, kept_values = forward(inputs, route_ids, weights)
        return (micro_index, output.astype(jnp.bfloat16), kept_values)

    micro_index, sent_rows, kept_values = forward_tick(
        0, jnp.zeros((row_count, model_width), jnp.bfloat16)
    )
    outputs = (
        jnp.zeros((micro_count, row_count, model_width), jnp.bfloat16)
        .at[micro_index]
        .set(sent_rows)
    )
    stacks = jax.tree.map(
        lambda leaf_array: jnp.zeros((micro_count,) + leaf_array.shape, leaf_array.dtype)
        .at[micro_index]
        .set(leaf_array),
        kept_values,
    )

    def forward_step(tick_index, loop_state):
        sent_rows, outputs, stacks = loop_state
        received = shifted_2(sent_rows, "pipe", 1)
        micro_index, sent_rows, kept_values = forward_tick(tick_index, received)
        outputs = outputs.at[micro_index].set(sent_rows)
        stacks = jax.tree.map(
            lambda whole_stack, leaf_array: whole_stack.at[micro_index].set(leaf_array),
            stacks,
            kept_values,
        )
        return (sent_rows, outputs, stacks)

    sent_rows, outputs, stacks = lax.fori_loop(
        1, micro_count + 1, forward_step, (sent_rows, outputs, stacks)
    )
    weights_back = (
        lax.all_gather(g_attn[0], "dp", axis=0, tiled=True),
        lax.all_gather(w_qkv[0], "dp", axis=0, tiled=True),
        lax.all_gather(w_out[0], "dp", axis=0, tiled=True),
        lax.all_gather(g_moe[0], "dp", axis=0, tiled=True),
        lax.all_gather(w_router[0], "dp", axis=0, tiled=True),
        lax.all_gather(w_in[0], "dp", axis=1, tiled=True),
        lax.all_gather(w_down[0], "dp", axis=1, tiled=True),
    )

    def backward_tick(tick_index, received, stacks):
        offset = tick_index - 1 + section_index
        micro_index = jnp.clip(offset, 0, micro_count - 1)
        is_valid = (offset >= 0) & (offset < micro_count)
        own_rows = lax.dynamic_index_in_dim(cotangent, micro_index, 0, keepdims=False).astype(
            jnp.float32
        )
        grad_rows = jnp.where(first_section, received.astype(jnp.float32), own_rows)
        grad_rows = jnp.where(is_valid, grad_rows, 0.0)
        kept_values = jax.tree.map(
            lambda whole_stack: lax.dynamic_index_in_dim(
                whole_stack, micro_index, 0, keepdims=False
            ),
            stacks,
        )
        grad_inputs, weight_grads = backward(grad_rows, kept_values, weights_back)
        return (micro_index, is_valid, grad_inputs, weight_grads)

    def store_grad(grad_store, micro_index, is_valid, grad_inputs):
        rounded = lax.optimization_barrier(grad_inputs.astype(jnp.bfloat16)).astype(jnp.float32)
        stored = jnp.where(first_section, grad_inputs, rounded)
        previous = lax.dynamic_index_in_dim(grad_store, micro_index, 0, keepdims=False)
        return grad_store.at[micro_index].set(jnp.where(is_valid, stored, previous))

    micro_index, is_valid, grad_inputs, totals = backward_tick(
        0, jnp.zeros((row_count, model_width), jnp.bfloat16), stacks
    )
    grad_store = store_grad(
        jnp.zeros((micro_count, row_count, model_width), jnp.float32),
        micro_index,
        is_valid,
        grad_inputs,
    )

    def backward_step(tick_index, loop_state):
        grad_inputs, grad_store, totals = loop_state
        received = shifted_2(grad_inputs.astype(jnp.bfloat16), "pipe", -1)
        micro_index, is_valid, grad_inputs, weight_grads = backward_tick(
            tick_index, received, stacks
        )
        grad_store = store_grad(grad_store, micro_index, is_valid, grad_inputs)
        totals = jax.tree.map(jnp.add, totals, weight_grads)
        return (grad_inputs, grad_store, totals)

    grad_inputs, grad_store, totals = lax.fori_loop(
        1, micro_count + 1, backward_step, (grad_inputs, grad_store, totals)
    )
    row_sums = lax.psum((totals[0], totals[3], totals[4]), "tensor")
    reduced = (
        lax.psum_scatter(
            row_sums[0].astype(jnp.bfloat16), "dp", scatter_dimension=0, tiled=True
        ).astype(jnp.float32),
        lax.psum_scatter(
            totals[1].astype(jnp.bfloat16), "dp", scatter_dimension=0, tiled=True
        ).astype(jnp.float32),
        lax.psum_scatter(
            totals[2].astype(jnp.bfloat16), "dp", scatter_dimension=0, tiled=True
        ).astype(jnp.float32),
        lax.psum_scatter(
            row_sums[1].astype(jnp.bfloat16), "dp", scatter_dimension=0, tiled=True
        ).astype(jnp.float32),
        lax.psum_scatter(
            row_sums[2].astype(jnp.bfloat16), "dp", scatter_dimension=0, tiled=True
        ).astype(jnp.float32),
        lax.psum_scatter(
            totals[5].astype(jnp.bfloat16), "dp", scatter_dimension=1, tiled=True
        ).astype(jnp.float32),
        lax.psum_scatter(
            totals[6].astype(jnp.bfloat16), "dp", scatter_dimension=1, tiled=True
        ).astype(jnp.float32),
    )
    return (
        outputs[None],
        grad_store[None],
        reduced[0][None],
        reduced[1][None],
        reduced[2][None],
        reduced[3][None],
        reduced[4][None],
        reduced[5][None],
        reduced[6][None],
    )


def solution(mesh):
    placed = (
        P("dp", "tensor", None),
        P("dp", "tensor", None),
        P("pipe", "dp", "tensor", None),
        P("pipe", "dp"),
        P("pipe", "dp", None, "tensor"),
        P("pipe", "dp", "tensor"),
        P("pipe", "dp"),
        P("pipe", "dp", None),
        P("pipe", None, "dp", "tensor"),
        P("pipe", None, "dp", "tensor"),
    )
    return jax.shard_map(
        on_device,
        mesh=mesh,
        in_specs=placed,
        out_specs=(
            P("pipe", "dp", "tensor", None),
            P("pipe", "dp", "tensor", None),
            P("pipe", "dp"),
            P("pipe", "dp", None, "tensor"),
            P("pipe", "dp", "tensor"),
            P("pipe", "dp"),
            P("pipe", "dp", None),
            P("pipe", None, "dp", "tensor"),
            P("pipe", None, "dp", "tensor"),
        ),
        check_vma=False,
    )
```

profile of v0, /device:TPU:0, one launch (start us, length us, event | category | flops | bytes accessed | tf_op | source)
XLA Modules:
  0.0 1228.4 jit_solution(5319572093360255714)
XLA Ops:
  11.7 68.2 %all-reduce.9 = (bf16[768]{0:T(1024)(128)(2,1)}, bf16[768]{0:T(1024)(128)(2,1)}) all-reduce(bf16[768]{0:T(1024)(128)(2,1)S(1)} %dynamic-update-slice.187, bf16[768]{0:T(1024)(128)(2,1)S(1)} %dynamic-update-slice.186), channel_id=6, replica_groups=mesh['pipe'=2,'dp'=32,'tensor'=2] {'dp'}, use_global_device_ids=true, to_apply=%add.1 | all-reduce | flops 1536 | bytes 6144 | tf_op jit(solution)/shard_map/all_gather | solution.py:280
  93.6 25.3 %all-gather.3 = bf16[1,768,384]{2,1,0:T(8,128)(2,1)} all-gather(bf16[1,24,384]{2,1,0:T(8,128)(2,1)} %param.93), channel_id=5, replica_groups=mesh['pipe'=2,'dp'=32,'tensor'=2] {'dp'}, dimensions={1}, use_global_device_ids=true | all-gather | bytes 608256 | tf_op jit(solution)/shard_map/all_gather | solution.py:279
  139.8 23.7 %all-gather.5 = bf16[1,768,4]{2,0,1:T(2,128)(2,1)S(1)} all-gather(bf16[1,24,4]{2,0,1:T(2,128)(2,1)S(1)} %copy.134), channel_id=7, replica_groups=mesh['pipe'=2,'dp'=32,'tensor'=2] {'dp'}, dimensions={1}, use_global_device_ids=true | all-gather | bytes 6336 | tf_op jit(solution)/shard_map/all_gather | solution.py:281
  190.0 9.8 all_gather.97
  214.3 50.2 %all-gather.19.cloned.1.call-done = bf16[1,4,768,1536]{3,2,1,0:T(8,128)(2,1)} async-done(((bf16[1,4,24,1536]{3,2,1,0:T(8,128)(2,1)}), bf16[1,4,768,1536]{3,2,1,0:T(8,128)(2,1)}) %all-gather.19.cloned.1.call-update) | async-done | bytes 9437200 | tf_op jit(solution)/shard_map/all_gather | solution.py:283
  282.0 10.6 reduce-scatter.22.cloned.1.call-done
  298.0 209.3 %while.116 = (s32[]{:T(128)}, bf16[128,768]{1,0:T(8,128)(2,1)}, bf16[2,128,768]{2,1,0:T(8,128)(2,1)}, f32[2,128,768]{2,1,0:T(8,128)}, bf16[2,256,768]{2,1,0:T(8,...) while((s32[]{:T(128)}, bf16[128,768]{1,0:T(8,128)(2,1)}, ...), condition=%wide.region_31.33_spmd, body=%wide.region_15.32_spmd.sunk | while | flops 2557593344 | bytes 71390216 | solution.py:323
  522.6 11.5 fusion.220
  549.6 9.3 fusion.255
  589.1 10.6 reduce-scatter.26.cloned.1.call-done
  607.0 228.0 %while.117 = (s32[]{:T(128)}, f32[128,768]{1,0:T(8,128)}, f32[2,128,768]{2,1,0:T(8,128)}, f32[768]{0:T(1024)}, f32[768,3,384]{2,0,1:T(8,128)}, /*index=5*/f32[76...) while((s32[]{:T(128)}, f32[128,768]{1,0:T(8,128)}, ...), condition=%wide.region_57.59_spmd, body=%wide.region_44.58_spmd.sunk | while | flops 5027098624 | bytes 225145872 | solution.py:380
  647.5 14.8 %convolution_add_fusion.16 = f32[4,768,1536]{2,1,0:T(8,128)} fusion(f32[4,768,1536]{2,1,0:T(8,128)} %get-tuple-element.3260, bf16[4,88,768]{2,1,0:T(8,128)(2,1)} %bitcast.877, f32[2,4,88,1536]{3,2,1,0:T(8,128)} %get-tuple-element.3306, s32[]{:T(128)} %min.42), kind=kOutput, calls=%fused_computation.4.clone.1 | convolution fusion | flops 870334464 | bytes 40452608 | tf_op jit(solution)/shard_map/while/body/eval_jaxpr/ecd,ecf->edf/dot_general | solution.py:178
  663.9 12.1 convolution_add_fusion.15
  705.3 10.0 reduce-scatter.40.cloned.1.call-done
  761.2 14.8 %convolution_add_fusion.16 = f32[4,768,1536]{2,1,0:T(8,128)} fusion(f32[4,768,1536]{2,1,0:T(8,128)} %get-tuple-element.3260, bf16[4,88,768]{2,1,0:T(8,128)(2,1)} %bitcast.877, f32[2,4,88,1536]{3,2,1,0:T(8,128)} %get-tuple-element.3306, s32[]{:T(128)} %min.42), kind=kOutput, calls=%fused_computation.4.clone.1 | convolution fusion | flops 870334464 | bytes 40452608 | tf_op jit(solution)/shard_map/while/body/eval_jaxpr/ecd,ecf->edf/dot_general | solution.py:178
  777.7 12.1 convolution_add_fusion.15
  819.0 10.0 reduce-scatter.40.cloned.1.call-done
  847.9 32.8 %copy.162 = bf16[4,768,1536]{2,0,1:T(4,128)(2,1)} copy(bf16[4,768,1536]{2,1,0:T(8,128)(2,1)S(1)} %convert_element_type.644) | data formatting | bytes 18874368
  880.7 10.5 copy.170
  898.3 32.8 %copy.164 = bf16[4,768,1536]{2,0,1:T(4,128)(2,1)} copy(bf16[4,768,1536]{2,1,0:T(8,128)(2,1)S(1)} %convert_element_type.645) | data formatting | bytes 18874368
  931.1 10.4 copy.171
  950.6 126.7 %all-reduce.8 = (bf16[768]{0:T(1024)(128)(2,1)S(1)}, bf16[768]{0:T(1024)(128)(2,1)S(1)}, bf16[768,4]{0,1:T(4,128)(2,1)S(1)}) all-reduce(bf16[768]{0:T(1024)(128)(2,1)S(1)} %get-tuple-element.2558, bf16[768]{0:T(1024)(128)(2,1)S(1)} %get-tuple-element.2559, ...), channel_id=19, replica_groups=mesh['pipe'=2,'dp'=32,'tensor'=2] {'dp'}, use_global_device_ids=true, to_apply=%region_59.61.clone | all-reduce | flops 4608 | bytes 18432
  1081.3 39.2 %reduce-scatter.28.cloned.1.call-done = bf16[24,6144]{1,0:T(8,128)(2,1)} async-done(((bf16[768,6144]{1,0:T(8,128)(2,1)}), bf16[24,6144]{1,0:T(8,128)(2,1)}) %reduce-scatter.28.cloned.1.call-update) | async-done | bytes 294928
  1122.6 97.0 %reduce-scatter.30.cloned.1.call-done = bf16[24,6144]{1,0:T(8,128)(2,1)} async-done(((bf16[768,6144]{1,0:T(8,128)(2,1)}), bf16[24,6144]{1,0:T(8,128)(2,1)}) %reduce-scatter.30.cloned.1.call-update) | async-done | bytes 294928
  (546 shorter events, 568.0 us)
Async XLA Ops:
  7.2 111.8 %all-gather.15.cloned.1.call-start = ((), (), s32[]{:S(2)}) async-start(), calls=%async_computation.15 | async-start | bytes 1824768 | tf_op jit(solution)/shard_map/all_gather | solution.py:278
  7.9 176.0 %reduce-scatter.20.cloned.1.call-start = ((), (), s32[]{:S(2)}) async-start(), calls=%async_computation.11 | async-start | bytes 1179648 | tf_op jit(solution)/shard_map/reduce_scatter | solution.py:95
  128.9 78.2 %all-gather.17.cloned.1.call-start = ((), (), s32[]{:S(2)}) async-start(), calls=%async_computation.16 | async-start | bytes 9732096 | tf_op jit(solution)/shard_map/all_gather | solution.py:282
  129.7 134.8 %all-gather.19.cloned.1.call-start = ((), (), s32[]{:S(2)}) async-start(), calls=%async_computation.17 | async-start | bytes 9732096 | tf_op jit(solution)/shard_map/all_gather | solution.py:283
  130.3 162.3 %reduce-scatter.22.cloned.1.call-start = ((), (), s32[]{:S(2)}) async-start(), calls=%async_computation.12 | async-start | bytes 589824 | tf_op jit(solution)/shard_map/reduce_scatter | solution.py:119
  131.0 54.1 %copy-start.30 = (f32[768]{0:T(1024)}, f32[768]{0:T(1024)S(1)}, u32[]{:S(2)}) copy-start(f32[768]{0:T(1024)S(1)} %convert_element_type.609) | copy-start | bytes 9220
  298.4 48.8 %reduce-scatter.34.cloned.1.call-start = ((), (), s32[]{:S(2)}) async-start(), calls=%async_computation.22 | async-start | bytes 1179648 | tf_op jit(solution)/shard_map/while/body/eval_jaxpr/reduce_scatter | solution.py:95
  298.4 12.7 %collective-permute-start = (bf16[128,768]{1,0:T(8,128)(2,1)}, bf16[128,768]{1,0:T(8,128)(2,1)S(1)}, u32[]{:S(2)}, u32[]{:S(2)}) collective-permute-start(bf16[128,768]{1,0:T(8,128)(2,1)} %get-tuple-element.3139), channel_id=1, source_target_pairs={{0,64},{1,65},{2,66},{3,67},{4,68},{5,69},{6,70},{7,71},{8,72},{9,... | collective-permute-start | bytes 589832 | tf_op jit(solution)/shard_map/while/body/eval_jaxpr/ppermute | solution.py:20
  325.3 72.6 %reduce-scatter.36.cloned.1.call-start = ((), (), s32[]{:S(2)}) async-start(), calls=%async_computation.23 | async-start | bytes 589824 | tf_op jit(solution)/shard_map/while/body/eval_jaxpr/reduce_scatter | solution.py:119
  402.8 48.7 %reduce-scatter.34.cloned.1.call-start = ((), (), s32[]{:S(2)}) async-start(), calls=%async_computation.22 | async-start | bytes 1179648 | tf_op jit(solution)/shard_map/while/body/eval_jaxpr/reduce_scatter | solution.py:95
  402.8 12.7 %collective-permute-start = (bf16[128,768]{1,0:T(8,128)(2,1)}, bf16[128,768]{1,0:T(8,128)(2,1)S(1)}, u32[]{:S(2)}, u32[]{:S(2)}) collective-permute-start(bf16[128,768]{1,0:T(8,128)(2,1)} %get-tuple-element.3139), channel_id=1, source_target_pairs={{0,64},{1,65},{2,66},{3,67},{4,68},{5,69},{6,70},{7,71},{8,72},{9,... | collective-permute-start | bytes 589832 | tf_op jit(solution)/shard_map/while/body/eval_jaxpr/ppermute | solution.py:20
  429.8 72.6 %reduce-scatter.36.cloned.1.call-start = ((), (), s32[]{:S(2)}) async-start(), calls=%async_computation.23 | async-start | bytes 589824 | tf_op jit(solution)/shard_map/while/body/eval_jaxpr/reduce_scatter | solution.py:119
  507.2 55.9 %reduce-scatter.24.cloned.1.call-start = ((), (), s32[]{:S(2)}) async-start(), calls=%async_computation.13 | async-start | bytes 589824 | tf_op jit(solution)/shard_map/reduce_scatter | solution.py:189
  546.5 53.2 %reduce-scatter.26.cloned.1.call-start = ((), (), s32[]{:S(2)}) async-start(), calls=%async_computation.14 | async-start | bytes 589824 | tf_op jit(solution)/shard_map/reduce_scatter | solution.py:253
  607.4 68.6 %reduce-scatter.38.cloned.1.call-start = ((), (), s32[]{:S(2)}) async-start(), calls=%async_computation.24 | async-start | bytes 589824 | tf_op jit(solution)/shard_map/while/body/eval_jaxpr/reduce_scatter | solution.py:189
  608.5 12.8 %collective-permute-start.1 = (bf16[128,768]{1,0:T(8,128)(2,1)S(1)}, bf16[128,768]{1,0:T(8,128)(2,1)S(1)}, u32[]{:S(2)}, u32[]{:S(2)}) collective-permute-start(bf16[128,768]{1,0:T(8,128)(2,1)S(1)} %convert_element_type.869), channel_id=1, source_target_pairs={{64,0},{65,1},{66,2},{67,3},{68,4},{69,5},{70,6},{71,7},{72,8},{73... | collective-permute-start | bytes 589832 | tf_op jit(solution)/shard_map/while/body/eval_jaxpr/ppermute | solution.py:20
  647.5 67.8 %reduce-scatter.40.cloned.1.call-start = ((), (), s32[]{:S(2)}) async-start(), calls=%async_computation.25 | async-start | bytes 589824 | tf_op jit(solution)/shard_map/while/body/eval_jaxpr/reduce_scatter | solution.py:253
  721.2 68.6 %reduce-scatter.38.cloned.1.call-start = ((), (), s32[]{:S(2)}) async-start(), calls=%async_computation.24 | async-start | bytes 589824 | tf_op jit(solution)/shard_map/while/body/eval_jaxpr/reduce_scatter | solution.py:189
  722.2 12.8 %collective-permute-start.1 = (bf16[128,768]{1,0:T(8,128)(2,1)S(1)}, bf16[128,768]{1,0:T(8,128)(2,1)S(1)}, u32[]{:S(2)}, u32[]{:S(2)}) collective-permute-start(bf16[128,768]{1,0:T(8,128)(2,1)S(1)} %convert_element_type.869), channel_id=1, source_target_pairs={{64,0},{65,1},{66,2},{67,3},{68,4},{69,5},{70,6},{71,7},{72,8},{73... | collective-permute-start | bytes 589832 | tf_op jit(solution)/shard_map/while/body/eval_jaxpr/ppermute | solution.py:20
  761.2 67.8 %reduce-scatter.40.cloned.1.call-start = ((), (), s32[]{:S(2)}) async-start(), calls=%async_computation.25 | async-start | bytes 589824 | tf_op jit(solution)/shard_map/while/body/eval_jaxpr/reduce_scatter | solution.py:253
  835.0 243.5 %all-reduce.12.cloned.1.call-start = ((), (), s32[]{:S(2)}) async-start(), calls=%async_computation.20 | async-start | bytes 3538944
  838.5 241.5 %reduce-scatter.32.cloned.1.call-start = ((), (), s32[]{:S(2)}) async-start(), calls=%async_computation.21 | async-start | bytes 608256
  840.6 279.9 %reduce-scatter.28.cloned.1.call-start = ((), (), s32[]{:S(2)}) async-start(), calls=%async_computation.18 | async-start | bytes 9732096
  891.2 328.4 %reduce-scatter.30.cloned.1.call-start = ((), (), s32[]{:S(2)}) async-start(), calls=%async_computation.19 | async-start | bytes 9732096
  (62 other events, 560.1 us)
Sparse Core Ops, SparseCore 0:
  10.4 45.8 all-gather.14
  129.0 20.9 reduce-scatter.19
  152.6 54.4 all-gather.16
  209.5 54.9 all-gather.18
  275.6 16.9 reduce-scatter.21
  325.5 21.6 reduce-scatter.33
  381.4 16.5 reduce-scatter.35
  429.9 21.6 reduce-scatter.33
  485.8 16.4 reduce-scatter.35
  546.6 16.4 reduce-scatter.23
  583.2 16.4 reduce-scatter.25
  647.6 17.7 reduce-scatter.37
  697.6 17.6 reduce-scatter.39
  761.3 17.7 reduce-scatter.37
  811.3 17.6 reduce-scatter.39
  838.9 104.5 all-reduce.11
  947.4 74.7 reduce-scatter.31
  1025.8 94.7 reduce-scatter.27
  1124.8 94.7 reduce-scatter.29
where the time goes:
time: 1240 us; the launch traced here: 1230 us
  blocking collectives  372 us (30%)
  waiting for transfers between devices  259 us (21%)
  matrix products  226 us (18%)
  other arithmetic  189 us (15%)
  local copies, waits for them, and re-layouts  157 us (13%)
  between operations  15.9 us (1%)
    unnamed x15, waiting for transfers between devices  138 us
    unnamed x1, blocking collectives  127 us
    unnamed x66, local copies, waits for them, and re-layouts  93.4 us
    all_gather x1, blocking collectives, on_device(): lax.all_gather(g_moe[0], 'dp', axis=0, tiled=True)  68.2 us
    scatter x22, other arithmetic, forward_step(): whole_stack.at[micro_index].set(leaf_array)  51.8 us
    all_gather x1, waiting for transfers between devices, on_device(): lax.all_gather(w_down[0], 'dp', axis=1, tiled=True)  50.2 us
    dot_general x3, matrix products, backward(): jnp.einsum('ecd,ecf->edf', grad_slots, activated.astype(jnp.bfloat16), pr...  41.2 us
    dot_general x3, matrix products, backward(): jnp.einsum('ecd,ecf->edf', filled, grad_hidden, preferred_element_type=jn...  33.5 us
  transfers between devices with their start and end apart: 23, of which 13 were waited for; matrix products, arithmetic and copies ran while one was open for 28% of the time, Pallas kernels for 0%

commit v1 on v0

v1 whole, which is shorter than its diff:
```python
import math

import jax
import jax.numpy as jnp
from jax import lax
from jax.sharding import Mesh
from jax.sharding import PartitionSpec as P

D = 768
DH = 64
E = 4
LEN = 256
HALF = 128
PAD = 96
QKV = 1152
OUT = 384
SMALL = 256
ATTN = QKV + OUT + SMALL
FFH = 1536

norm_eps = 1e-06
f32 = jnp.float32
bf16 = jnp.bfloat16
COLUMN = ("pipe", "core", "tensor")


def column_pairs(target):
    pairs = []
    for p in range(2):
        for c in range(2):
            for t in range(2):
                p2, c2, t2 = target(p, c, t)
                pairs.append((p * 4 + c * 2 + t, p2 * 4 + c2 * 2 + t2))
    return pairs


def column_send(array, target):
    return lax.ppermute(array, COLUMN, column_pairs(target))


def core_swap(array):
    return lax.ppermute(array, "core", [(0, 1), (1, 0)])


def chip_swap(array, k):
    return lax.ppermute(array, ("pipe", "tensor"), [(i, i ^ k) for i in range(4)])


def axis_swap(array, axis, k):
    return lax.ppermute(array, axis, [(i, i ^ k) for i in range(4)])


def gather_axis(block, axis, dim):
    me = lax.axis_index(axis)
    whole = jnp.zeros(block.shape[:dim] + (4,) + block.shape[dim:], block.dtype)
    parts = [block] + [axis_swap(block, axis, k) for k in (1, 2, 3)]
    for k, part in enumerate(parts):
        whole = lax.dynamic_update_index_in_dim(whole, part, me ^ k, dim)
    return whole


def gather_plane(block, first):
    rows, width = block.shape
    if first == "x":
        whole = gather_axis(gather_axis(block, "x", 0), "y", 1)
    else:
        whole = gather_axis(gather_axis(block, "y", 0), "x", 0)
    return whole.reshape(16 * rows, width)


def scatter_axis(whole, axis, dim):
    me = lax.axis_index(axis)
    parts = [lax.dynamic_index_in_dim(whole, me ^ k, dim, keepdims=False) for k in range(4)]
    got = [parts[0]] + [axis_swap(parts[k], axis, k) for k in (1, 2, 3)]
    return sum(part.astype(f32) for part in got).astype(bf16)


def scatter_plane(whole, first):
    whole = whole.reshape(4, 4, -1, whole.shape[1])
    if first == "x":
        return scatter_axis(scatter_axis(whole, "x", 0), "y", 0)
    return scatter_axis(scatter_axis(whole, "y", 1), "x", 0)


def rms_scale(values):
    return lax.rsqrt(jnp.mean(values * values, axis=-1, keepdims=True) + norm_eps)


def norm_back(grad_normed, values, scale_rows, gain):
    normal = values * scale_rows
    weighted = grad_normed * gain
    grad_values = scale_rows * (
        weighted - normal * jnp.mean(weighted * normal, axis=-1, keepdims=True)
    )
    return grad_values, jnp.sum(grad_normed * normal, axis=0)


def matmul(left, right, dims):
    return lax.dot_general(left, right, ((dims[:1], dims[1:]), ((), ())), preferred_element_type=f32)


def pair_sum(partial):
    mine = partial.astype(bf16)
    return mine.astype(f32) + core_swap(mine).astype(f32)


def to_experts(rows):
    parts = [rows[k * PAD : (k + 1) * PAD] for k in range(4)]
    return jnp.concatenate([parts[0]] + [chip_swap(parts[k], k) for k in (1, 2, 3)], axis=0)


def unpack(packed):
    return [
        packed[:, i * OUT : (i + 1) * OUT].astype(bf16).reshape(LEN, OUT // DH, DH)
        for i in range(3)
    ]


def forward(inputs, table, onehot, weights):
    w_qkv, w_out, g_attn, g_moe, w_router, w_in, w_down = weights
    score_scale = 1.0 / math.sqrt(DH)
    scale_in = rms_scale(inputs)
    normed = (inputs * scale_in * g_attn).astype(bf16)
    query, key, value = unpack(matmul(normed, w_qkv, (1, 0)))
    scores = jnp.einsum("qhd,khd->hqk", query, key, preferred_element_type=f32) * score_scale
    top = jnp.max(scores, axis=-1, keepdims=True)
    exponent = jnp.exp(scores - top)
    probs = exponent / jnp.sum(exponent, axis=-1, keepdims=True)
    context = jnp.einsum("hqk,khd->qhd", probs.astype(bf16), value, preferred_element_type=f32)
    context = context.astype(bf16).reshape(LEN, OUT)
    middle = inputs + pair_sum(matmul(context, w_out, (1, 1)))
    scale_mid = rms_scale(middle)
    mixed = (middle * scale_mid * g_moe).astype(bf16)
    logits = matmul(mixed, w_router, (1, 0))
    exponent = jnp.exp(logits - jnp.max(logits, axis=-1, keepdims=True))
    router_probs = exponent / jnp.sum(exponent, axis=-1, keepdims=True)
    gate = jnp.sum(onehot * router_probs, axis=-1, keepdims=True)
    filled = to_experts(matmul(table, mixed, (1, 0)).astype(bf16))
    hidden = matmul(filled, w_in, (1, 0))
    cdf = 0.5 * (1.0 + lax.erf(hidden * (1.0 / math.sqrt(2.0))))
    activated = (hidden * cdf).astype(bf16)
    slope = cdf + hidden * jnp.exp(-0.5 * hidden * hidden) * (1.0 / math.sqrt(2.0 * math.pi))
    expert_out = to_experts(matmul(activated, w_down, (1, 1)).astype(bf16))
    combined = pair_sum(matmul(table, expert_out, (0, 0)))
    output = (middle + gate * combined).astype(bf16)
    kept = (
        inputs, scale_in, normed, query, key, value, probs, context, middle, scale_mid,
        mixed, router_probs, gate, filled, activated, slope, combined,
    )
    return output, kept


def backward_moe(grad_out, kept, table, onehot, weights):
    w_qkv, w_out, g_attn, g_moe, w_router, w_in, w_down = weights
    (
        inputs, scale_in, normed, query, key, value, probs, context, middle, scale_mid,
        mixed, router_probs, gate, filled, activated, slope, combined,
    ) = kept
    grad_gate = jnp.sum(grad_out * combined, axis=-1, keepdims=True)
    grad_branch = (gate * grad_out).astype(bf16)
    grad_slots = to_experts(matmul(table, grad_branch, (1, 0)).astype(bf16))
    grad_act = matmul(grad_slots, w_down, (1, 0))
    grad_hidden = (grad_act * slope).astype(bf16)
    grad_filled = to_experts(matmul(grad_hidden, w_in, (1, 1)).astype(bf16))
    grad_w_down = matmul(grad_slots, activated, (0, 0)).astype(bf16)
    grad_w_in = matmul(filled, grad_hidden, (0, 0)).astype(bf16)
    grad_mixed = pair_sum(matmul(table, grad_filled, (0, 0)))
    grad_logits = router_probs * (onehot - gate) * grad_gate
    grad_w_router = lax.dot_general(
        mixed.astype(f32), grad_logits, (((0,), (0,)), ((), ())), precision=lax.Precision.HIGHEST
    )
    back_rows = sum(grad_logits[:, e : e + 1] * w_router[:, e].astype(f32)[None, :] for e in range(E))
    grad_norm, grad_g_moe = norm_back(grad_mixed + back_rows, middle, scale_mid, g_moe)
    return grad_out + grad_norm, grad_w_in, grad_w_down, grad_w_router, grad_g_moe


def backward_attn(grad_middle, kept, weights):
    w_qkv, w_out, g_attn, g_moe, w_router, w_in, w_down = weights
    (
        inputs, scale_in, normed, query, key, value, probs, context, middle, scale_mid,
        mixed, router_probs, gate, filled, activated, slope, combined,
    ) = kept
    score_scale = 1.0 / math.sqrt(DH)
    proj = grad_middle.astype(bf16)
    grad_heads = matmul(proj, w_out, (1, 0)).astype(bf16).reshape(LEN, OUT // DH, DH)
    grad_value = jnp.einsum(
        "hqk,qhd->khd", probs.astype(bf16), grad_heads, preferred_element_type=f32
    ).astype(bf16)
    grad_probs = jnp.einsum("qhd,khd->hqk", grad_heads, value, preferred_element_type=f32)
    grad_scores = (
        probs * (grad_probs - jnp.sum(grad_probs * probs, axis=-1, keepdims=True))
    ).astype(bf16)
    grad_query = (
        jnp.einsum("hqk,khd->qhd", grad_scores, key, preferred_element_type=f32) * score_scale
    ).astype(bf16)
    grad_key = (
        jnp.einsum("hqk,qhd->khd", grad_scores, query, preferred_element_type=f32) * score_scale
    ).astype(bf16)
    packed = jnp.concatenate(
        [grad_query.reshape(LEN, OUT), grad_key.reshape(LEN, OUT), grad_value.reshape(LEN, OUT)],
        axis=1,
    )
    grad_normed = pair_sum(matmul(packed, w_qkv, (1, 1)))
    grad_w_out = matmul(proj, context, (0, 0)).astype(bf16)
    grad_w_qkv = matmul(normed, packed, (0, 0)).astype(bf16)
    grad_norm, grad_g_attn = norm_back(grad_normed, inputs, scale_in, g_attn)
    return grad_middle + grad_norm, grad_w_qkv, grad_w_out, grad_g_attn


def by_layer(p, near, far):
    return jnp.where(p == 0, near, far), jnp.where(p == 0, far, near)


def on_device(tokens, cotangent, routes, g_attn, w_qkv, w_out, g_moe, w_router, w_in, w_down):
    p, c, t = lax.axis_index("pipe"), lax.axis_index("core"), lax.axis_index("tensor")
    chip = p * 2 + t

    def spread(chunk_of):
        got = []
        for k in range(4):
            k1, k0 = k >> 1, k & 1
            got.append(column_send(chunk_of(k), lambda p, c, t: (p ^ k1, t, c ^ k0)))
        layers = []
        for first, second in ((by_layer(p, got[0], got[2])), (by_layer(p, got[1], got[3]))):
            layers.append((first, second))
        return [
            jnp.concatenate(
                [
                    jnp.where(t == 0, layers[0][l], layers[1][l]),
                    jnp.where(t == 0, layers[1][l], layers[0][l]),
                ],
                axis=0,
            )
            for l in range(2)
        ]

    def expert_chunk(k):
        expert = (p * 2 + c) ^ k
        return jnp.concatenate(
            [
                lax.dynamic_index_in_dim(w_in[0], expert, 0, keepdims=False),
                lax.dynamic_index_in_dim(w_down[0], expert, 0, keepdims=False),
            ],
            axis=1,
        )

    moe_blocks = spread(expert_chunk)
    small = jnp.concatenate([g_attn[0][:, None], g_moe[0][:, None], w_router[0]], axis=1)
    small = jnp.pad(small, ((0, 0), (0, SMALL - small.shape[1])))
    attn_chunk = jnp.concatenate([w_qkv[0].reshape(-1, QKV), w_out[0], small], axis=1)
    attn_blocks = spread(lambda k: attn_chunk)

    def to_owner(rows):
        got = [column_send(rows, lambda p, c, t, j=j: (p, t ^ j, c)) for j in range(2)]
        return jnp.where(c == 0, got[0], got[1]), jnp.where(c == 0, got[1], got[0])

    own_routes = routes[0, :, :, 0].astype(bf16)
    far_routes = lax.ppermute(own_routes, "pipe", [(0, 1), (1, 0)])
    route_pair = jnp.stack(by_layer(p, own_routes, far_routes))
    route_rows = lax.dynamic_index_in_dim(route_pair, p, 1, keepdims=False)
    own_tokens = lax.dynamic_index_in_dim(tokens, p, 0, keepdims=False)
    extra = jnp.pad(route_rows.reshape(1, 2 * HALF), ((0, 15), (0, D - 2 * HALF)))
    low_rows, high_rows = to_owner(jnp.concatenate([own_tokens, extra], axis=0))
    inputs = jnp.concatenate([low_rows[:HALF], high_rows[:HALF]], axis=0).astype(f32)
    tables, onehots = [], []
    earlier = (
        lax.broadcasted_iota(jnp.int32, (LEN, LEN), 0)
        < lax.broadcasted_iota(jnp.int32, (LEN, LEN), 1)
    ).astype(bf16)
    for l in range(2):
        cut = slice(l * HALF, (l + 1) * HALF)
        ids = jnp.concatenate([low_rows[HALF, cut], high_rows[HALF, cut]]).astype(jnp.int32)
        picks = (ids[None, :] == jnp.arange(E, dtype=jnp.int32)[:, None]).astype(f32)
        before = matmul(picks.astype(bf16), earlier, (1, 0))
        rank = jnp.sum(before * picks, axis=0).astype(jnp.int32)
        place = (ids ^ chip) * PAD + rank
        tables.append(
            (place[None, :] == jnp.arange(E * PAD, dtype=jnp.int32)[:, None]).astype(bf16)
        )
        onehots.append(picks.T)

    moe_full = lax.all_gather(
        jnp.concatenate(moe_blocks, axis=1), ("x", "y"), axis=0, tiled=True
    )
    attn_full = [gather_plane(attn_blocks[0], "x"), gather_plane(attn_blocks[1], "y")]

    def weights_of(attn, w_in_full, w_down_full):
        small = attn[:, QKV + OUT :]
        return (
            attn[:, :QKV],
            attn[:, QKV : QKV + OUT],
            small[:, 0].astype(f32)[None, :],
            small[:, 1].astype(f32)[None, :],
            small[:, 2 : 2 + E],
            w_in_full,
            w_down_full,
        )

    weights = [
        weights_of(
            attn_full[l],
            moe_full[:, 2 * l * FFH : (2 * l + 1) * FFH],
            moe_full[:, (2 * l + 1) * FFH : (2 * l + 2) * FFH],
        )
        for l in range(2)
    ]

    cot_rows = lax.dynamic_index_in_dim(cotangent, p, 0, keepdims=False)
    grad_out = jnp.concatenate(to_owner(cot_rows), axis=0).astype(f32)

    first_out, kept_first = forward(inputs, tables[0], onehots[0], weights[0])
    second_out, kept_second = forward(first_out.astype(f32), tables[1], onehots[1], weights[1])

    def to_home(first, second):
        cut = lambda rows: lax.dynamic_slice_in_dim(rows, c * HALF, HALF, 0)
        near, far = by_layer(p, cut(first), cut(second))
        near = column_send(near, lambda p, c, t: (p, t, c))
        far = column_send(far, lambda p, c, t: (1 - p, t, c))
        return jnp.stack(by_layer(p, near, far))

    hidden_states = to_home(first_out, second_out)

    def small_grads(grad_g_attn, grad_g_moe, grad_w_router):
        rows = jnp.concatenate([grad_g_attn[:, None], grad_g_moe[:, None], grad_w_router], axis=1)
        return jnp.pad(rows, ((0, 0), (0, SMALL - rows.shape[1]))).astype(bf16)

    grad_mid, g_in, g_down, g_router, gg_moe = backward_moe(
        grad_out, kept_second, tables[1], onehots[1], weights[1]
    )
    grad_x, g_qkv, g_out, gg_attn = backward_attn(grad_mid, kept_second, weights[1])
    second_grad = grad_x.astype(bf16)
    second_parts = [g_qkv, g_out, small_grads(gg_attn, gg_moe, g_router), g_in, g_down]
    grad_mid, g_in, g_down, g_router, gg_moe = backward_moe(
        second_grad.astype(f32), kept_first, tables[0], onehots[0], weights[0]
    )
    reduced = lax.psum_scatter(
        jnp.concatenate(second_parts + [g_in, g_down], axis=1),
        ("x", "y"), scatter_dimension=0, tiled=True,
    )
    reduced = lax.optimization_barrier(reduced)
    grad_x, g_qkv, g_out, gg_attn = backward_attn(grad_mid, kept_first, weights[0])
    attn_first = jnp.concatenate(
        [
            scatter_plane(g_qkv[:, : 2 * OUT], "x"),
            scatter_plane(
                jnp.concatenate(
                    [g_qkv[:, 2 * OUT :], g_out, small_grads(gg_attn, gg_moe, g_router)], axis=1
                ),
                "y",
            ),
        ],
        axis=1,
    )
    grad_inputs = to_home(grad_x.astype(bf16), second_grad).astype(f32)

    near, far = by_layer(
        p,
        jnp.concatenate([attn_first, reduced[:, ATTN + 2 * FFH :]], axis=1),
        reduced[:, : ATTN + 2 * FFH],
    )
    attn_sum = jnp.zeros((24, ATTN), f32)
    moe_all = jnp.zeros((E, 24, 2 * FFH), bf16)
    for k in range(4):
        k1, k0 = k >> 1, k & 1
        layer_rows = far if k1 else near
        piece = lax.dynamic_slice_in_dim(layer_rows, (t ^ k0) * 24, 24, 0)
        got = column_send(piece, lambda p, c, t: (p ^ k1, t ^ k0, c))
        attn_sum = attn_sum + got[:, :ATTN].astype(f32)
        moe_all = lax.dynamic_update_index_in_dim(moe_all, got[:, ATTN:], (p * 2 + c) ^ k, 0)
    small = attn_sum[:, QKV + OUT :]
    return (
        hidden_states[None],
        grad_inputs[None],
        small[:, 0][None],
        attn_sum[:, :QKV].reshape(24, 3, OUT)[None],
        attn_sum[:, QKV : QKV + OUT][None],
        small[:, 1][None],
        small[:, 2 : 2 + E][None],
        moe_all[:, :, :FFH].astype(f32)[None],
        moe_all[:, :, FFH:].astype(f32)[None],
    )


def solution(mesh):
    grid = Mesh(mesh.devices.reshape(2, 4, 4, 2, 2), ("pipe", "x", "y", "core", "tensor"))
    dp = ("x", "y", "core")
    return jax.shard_map(
        on_device,
        mesh=grid,
        in_specs=(
            P(dp, "tensor", None),
            P(dp, "tensor", None),
            P("pipe", dp, "tensor", None),
            P("pipe", dp),
            P("pipe", dp, None, "tensor"),
            P("pipe", dp, "tensor"),
            P("pipe", dp),
            P("pipe", dp, None),
            P("pipe", None, dp, "tensor"),
            P("pipe", None, dp, "tensor"),
        ),
        out_specs=(
            P("pipe", dp, "tensor", None),
            P("pipe", dp, "tensor", None),
            P("pipe", dp),
            P("pipe", dp, None, "tensor"),
            P("pipe", dp, "tensor"),
            P("pipe", dp),
            P("pipe", dp, None),
            P("pipe", None, dp, "tensor"),
            P("pipe", None, dp, "tensor"),
        ),
        check_vma=False,
    )
```

time: 1240 us -> 452 us (0.36)
  blocking collectives: 372 us -> 0 us
  other arithmetic: 189 us -> 24.1 us
  matrix products: 226 us -> 69.7 us
  local copies, waits for them, and re-layouts: 157 us -> 39.6 us
  starting transfers between devices: 8.41 us -> 108 us
  waiting for transfers between devices: 259 us -> 185 us
    all_gather x18 -> x0, blocking collectives: 237 us -> none  [the longest x1 68.2 us: on_device(): lax.all_gather(g_moe[0], 'dp', axis=0, tiled=True)]
    ppermute x4 -> x77, waiting for transfers between devices: 0.01 us -> 180 us  [the longest x24 134 us: axis_swap(): return lax.ppermute(array, axis, [(i, i ^ k) for i in range(4)])]
    dot_general x72 -> x48, matrix products: 226 us -> 66 us  [the longest x36 55.8 us: matmul(): lax.dot_general(left, right, ((dims[:1], dims[1:]), ((), ())), preferred_...]
    unnamed x15 -> x2, waiting for transfers between devices: 138 us -> 0.03 us
    unnamed x1 -> x0, blocking collectives: 127 us -> none
    ppermute x4 -> x77, starting transfers between devices: 7.71 us -> 108 us  [the longest x24 37.8 us: chip_swap(): lax.ppermute(array, ('pipe', 'tensor'), [(i, i ^ k) for i in range(4)])]
    unnamed x66 -> x253, local copies, waits for them, and re-layouts: 93.4 us -> 12.1 us
    scatter x36 -> x0, other arithmetic: 78.2 us -> none  [the longest x22 51.8 us: forward_step(): whole_stack.at[micro_index].set(leaf_array)]
  transfers between devices with their start and end apart: 23 -> 79, of which waited for: 13 -> 35; matrix products, arithmetic and copies ran while one was open for 28% -> 17% of each run, Pallas kernels for 0% -> 0%
where the time goes in v1:
time: 452 us; the launch traced here: 443 us
  waiting for transfers between devices  185 us (41%)
  starting transfers between devices  108 us (24%)
  matrix products  69.7 us (15%)
  local copies, waits for them, and re-layouts  39.6 us (9%)
  other arithmetic  24.1 us (5%)
  between operations  16.8 us (4%)
    ppermute x24, waiting for transfers between devices, axis_swap(): return lax.ppermute(array, axis, [(i, i ^ k) for i in range(4)])  134 us
    dot_general x36, matrix products, matmul(): lax.dot_general(left, right, ((dims[:1], dims[1:]), ((), ())), preferred_...  55.8 us
    ppermute x24, starting transfers between devices, chip_swap(): lax.ppermute(array, ('pipe', 'tensor'), [(i, i ^ k) for i in range(4)])  37.8 us
    ppermute x24, starting transfers between devices, axis_swap(): return lax.ppermute(array, axis, [(i, i ^ k) for i in range(4)])  34.5 us
    ppermute x20, starting transfers between devices, column_send(): return lax.ppermute(array, COLUMN, column_pairs(target))  33 us
    ppermute x24, waiting for transfers between devices, chip_swap(): lax.ppermute(array, ('pipe', 'tensor'), [(i, i ^ k) for i in range(4)])  26.6 us
    ppermute x20, waiting for transfers between devices, column_send(): return lax.ppermute(array, COLUMN, column_pairs(target))  13 us
    unnamed x253, local copies, waits for them, and re-layouts  12.1 us
  transfers between devices with their start and end apart: 79, of which 35 were waited for; matrix products, arithmetic and copies ran while one was open for 17% of the time, Pallas kernels for 0%

profile of v1, /device:TPU:0, one launch (start us, length us, event | category | flops | bytes accessed | tf_op | source)
XLA Modules:
  0.0 443.0 jit_solution(7489033417873913562)
XLA Ops:
  8.5 4.2 collective-permute-start.20
  13.6 3.9 collective-permute-start.19
  21.4 5.2 %collective-permute-start.6 = (bf16[24,1792]{1,0:T(8,128)(2,1)S(1)}, bf16[24,1792]{1,0:T(8,128)(2,1)S(1)}, u32[]{:S(2)}, u32[]{:S(2)}) collective-permute-start(bf16[24,1792]{1,0:T(8,128)(2,1)S(1)} %fusion.168), channel_id=1, source_target_pairs={{0,65},{1,67},{2,64},{3,66},{64,1},{65,3},{66,0},{67,2},{4,69},{5,... | collective-permute-start | bytes 258056 | tf_op jit(solution)/shard_map/ppermute | solution.py:38
  50.7 6.7 %collective-permute-done.25 = bf16[48,1792]{1,0:T(8,128)(2,1)S(1)} collective-permute-done((bf16[48,1792]{1,0:T(8,128)(2,1)S(1)}, bf16[48,1792]{1,0:T(8,128)(2,1)S(1)}, u32[]{:S(2)}, u32[]{:S(2)}) %collective-permute-start.25) | collective-permute-done | bytes 172064 | tf_op jit(solution)/shard_map/ppermute | solution.py:50
  59.7 6.0 %collective-permute-done.27 = bf16[48,1792]{1,0:T(8,128)(2,1)S(1)} collective-permute-done((bf16[48,1792]{1,0:T(8,128)(2,1)S(1)}, bf16[48,1792]{1,0:T(8,128)(2,1)S(1)}, u32[]{:S(2)}, u32[]{:S(2)}) %collective-permute-start.27) | collective-permute-done | bytes 172064 | tf_op jit(solution)/shard_map/ppermute | solution.py:50
  76.3 55.8 %collective-permute-done.10 = bf16[4,48,1792]{2,1,0:T(8,128)(2,1)S(1)} collective-permute-done((bf16[4,48,1792]{2,1,0:T(8,128)(2,1)S(1)}, bf16[4,48,1792]{2,1,0:T(8,128)(2,1)S(1)}, u32[]{:S(2)}, u32[]{:S(2)}) %collective-permute-start.10) | collective-permute-done | bytes 688160 | tf_op jit(solution)/shard_map/ppermute | solution.py:50
  135.0 14.2 %collective-permute-done.12 = bf16[4,48,1792]{2,1,0:T(8,128)(2,1)S(1)} collective-permute-done((bf16[4,48,1792]{2,1,0:T(8,128)(2,1)S(1)}, bf16[4,48,1792]{2,1,0:T(8,128)(2,1)S(1)}, u32[]{:S(2)}, u32[]{:S(2)}) %collective-permute-start.12) | collective-permute-done | bytes 688160 | tf_op jit(solution)/shard_map/ppermute | solution.py:50
  178.0 3.7 fusion.46
  182.4 4.2 collective-permute-start.21
  207.7 4.0 collective-permute-start.32
  222.6 4.0 fusion.52
  227.4 4.1 collective-permute-start.35
  244.3 4.3 collective-permute-done.46
  278.4 4.2 collective-permute-start.51
  292.5 3.9 fusion.4
  304.5 3.9 collective-permute-start.56
  335.8 11.0 %collective-permute-done.61 = bf16[4,48,768]{2,1,0:T(8,128)(2,1)S(1)} collective-permute-done((bf16[4,48,768]{2,1,0:T(8,128)(2,1)S(1)}, bf16[4,48,768]{2,1,0:T(8,128)(2,1)S(1)}, u32[]{:S(2)}, u32[]{:S(2)}) %collective-permute-start.61) | collective-permute-done | bytes 294944 | tf_op jit(solution)/shard_map/ppermute | solution.py:50
  349.1 11.6 %collective-permute-done.62 = bf16[4,48,768]{2,1,0:T(8,128)(2,1)S(1)} collective-permute-done((bf16[4,48,768]{2,1,0:T(8,128)(2,1)S(1)}, bf16[4,48,768]{2,1,0:T(8,128)(2,1)S(1)}, u32[]{:S(2)}, u32[]{:S(2)}) %collective-permute-start.62) | collective-permute-done | bytes 294944 | tf_op jit(solution)/shard_map/ppermute | solution.py:50
  368.8 3.7 collective-permute-done.65
  380.1 7.7 %collective-permute-done.67 = bf16[4,48,1024]{2,1,0:T(8,128)(2,1)S(1)} collective-permute-done((bf16[4,48,1024]{2,1,0:T(8,128)(2,1)S(1)}, bf16[4,48,1024]{2,1,0:T(8,128)(2,1)S(1)}, u32[]{:S(2)}, u32[]{:S(2)}) %collective-permute-start.67) | collective-permute-done | bytes 393248 | tf_op jit(solution)/shard_map/ppermute | solution.py:50
  387.8 9.8 %collective-permute-done.69 = bf16[4,48,1024]{2,1,0:T(8,128)(2,1)S(1)} collective-permute-done((bf16[4,48,1024]{2,1,0:T(8,128)(2,1)S(1)}, bf16[4,48,1024]{2,1,0:T(8,128)(2,1)S(1)}, u32[]{:S(2)}, u32[]{:S(2)}) %collective-permute-start.69) | collective-permute-done | bytes 393248 | tf_op jit(solution)/shard_map/ppermute | solution.py:50
  407.3 4.1 reduce-scatter.2.cloned.1.call-done
  414.4 4.9 %collective-permute-start.74 = (bf16[24,4864]{1,0:T(8,128)(2,1)S(1)}, bf16[24,4864]{1,0:T(8,128)(2,1)S(1)}, u32[]{:S(2)}, u32[]{:S(2)}) collective-permute-start(bf16[24,4864]{1,0:T(8,128)(2,1)S(1)} %get-tuple-element.135), channel_id=1, source_target_pairs={{0,2},{1,0},{2,3},{3,1},{64,66},{65,64},{66,67},{67,65},{4,6},{5,4... | collective-permute-start | bytes 700424 | tf_op jit(solution)/shard_map/ppermute | solution.py:38
  421.3 8.1 %collective-permute-done.74 = bf16[24,4864]{1,0:T(8,128)(2,1)S(1)} collective-permute-done((bf16[24,4864]{1,0:T(8,128)(2,1)S(1)}, bf16[24,4864]{1,0:T(8,128)(2,1)S(1)}, u32[]{:S(2)}, u32[]{:S(2)}) %collective-permute-start.74) | collective-permute-done | bytes 233504 | tf_op jit(solution)/shard_map/ppermute | solution.py:38
  (588 shorter events, 232.8 us)
Async XLA Ops:
  7.2 167.8 %all-gather.2.cloned.1.call-start = ((), (), s32[]{:S(2)}) async-start(), calls=%async_computation.1 | async-start | bytes 10027008 | tf_op jit(solution)/shard_map/all_gather | solution.py:282
  21.1 390.3 %reduce-scatter.2.cloned.1.call-start = ((), (), s32[]{:S(2)}) async-start(), calls=%async_computation.2 | async-start | bytes 12951552 | tf_op jit(solution)/shard_map/reduce_scatter | solution.py:336
  39.0 31.5 %collective-permute-start.8 = (bf16[48,1792]{1,0:T(8,128)(2,1)S(1)}, bf16[48,1792]{1,0:T(8,128)(2,1)S(1)}, u32[]{:S(2)}, u32[]{:S(2)}) collective-permute-start(bf16[48,1792]{1,0:T(8,128)(2,1)S(1)} %pad_maximum_fusion.13), channel_id=1, source_target_pairs={{0,32},{16,48},{32,0},{48,16},{1,33},{17,49},{33,1},{49,17},{2,34}... | collective-permute-start | bytes 516104 | tf_op jit(solution)/shard_map/ppermute | solution.py:50
  43.8 26.2 %collective-permute-start.7 = (bf16[48,1792]{1,0:T(8,128)(2,1)S(1)}, bf16[48,1792]{1,0:T(8,128)(2,1)S(1)}, u32[]{:S(2)}, u32[]{:S(2)}) collective-permute-start(bf16[48,1792]{1,0:T(8,128)(2,1)S(1)} %pad_maximum_fusion.13), channel_id=1, source_target_pairs={{0,16},{16,0},{32,48},{48,32},{1,17},{17,1},{33,49},{49,33},{2,18}... | collective-permute-start | bytes 516104 | tf_op jit(solution)/shard_map/ppermute | solution.py:50
  44.4 26.2 %collective-permute-start.9 = (bf16[48,1792]{1,0:T(8,128)(2,1)S(1)}, bf16[48,1792]{1,0:T(8,128)(2,1)S(1)}, u32[]{:S(2)}, u32[]{:S(2)}) collective-permute-start(bf16[48,1792]{1,0:T(8,128)(2,1)S(1)} %pad_maximum_fusion.13), channel_id=1, source_target_pairs={{0,48},{16,32},{32,16},{48,0},{1,49},{17,33},{33,17},{49,1},{2,50}... | collective-permute-start | bytes 516104 | tf_op jit(solution)/shard_map/ppermute | solution.py:50
  45.8 13.2 %collective-permute-start.26 = (bf16[48,1792]{1,0:T(8,128)(2,1)S(1)}, bf16[48,1792]{1,0:T(8,128)(2,1)S(1)}, u32[]{:S(2)}, u32[]{:S(2)}) collective-permute-start(bf16[48,1792]{1,0:T(8,128)(2,1)S(1)} %pad_maximum_fusion.14), channel_id=1, source_target_pairs={{0,8},{4,12},{8,0},{12,4},{1,9},{5,13},{9,1},{13,5},{2,10},{6,14},... | collective-permute-start | bytes 516104 | tf_op jit(solution)/shard_map/ppermute | solution.py:50
  66.4 101.4 %collective-permute-start.30 = (bf16[4,48,1792]{2,1,0:T(8,128)(2,1)}, bf16[4,48,1792]{2,1,0:T(8,128)(2,1)}, u32[]{:S(2)}, u32[]{:S(2)}) collective-permute-start(bf16[4,48,1792]{2,1,0:T(8,128)(2,1)} %bitcast_dynamic-update-slice_fusion.8), channel_id=1, source_target_pairs={{0,48},{16,32},{32,16},{48,0},{1,49},{17,33},{33,17},{49,1},{2,50}... | collective-permute-start | bytes 2064392 | tf_op jit(solution)/shard_map/ppermute | solution.py:50
  69.2 90.4 %collective-permute-start.29 = (bf16[4,48,1792]{2,1,0:T(8,128)(2,1)}, bf16[4,48,1792]{2,1,0:T(8,128)(2,1)}, u32[]{:S(2)}, u32[]{:S(2)}) collective-permute-start(bf16[4,48,1792]{2,1,0:T(8,128)(2,1)} %bitcast_dynamic-update-slice_fusion.8), channel_id=1, source_target_pairs={{0,32},{16,48},{32,0},{48,16},{1,33},{17,49},{33,1},{49,17},{2,34}... | collective-permute-start | bytes 2064392 | tf_op jit(solution)/shard_map/ppermute | solution.py:50
  70.0 87.6 %collective-permute-start.28 = (bf16[4,48,1792]{2,1,0:T(8,128)(2,1)}, bf16[4,48,1792]{2,1,0:T(8,128)(2,1)}, u32[]{:S(2)}, u32[]{:S(2)}) collective-permute-start(bf16[4,48,1792]{2,1,0:T(8,128)(2,1)} %bitcast_dynamic-update-slice_fusion.8), channel_id=1, source_target_pairs={{0,16},{16,0},{32,48},{48,32},{1,17},{17,1},{33,49},{49,33},{2,18}... | collective-permute-start | bytes 2064392 | tf_op jit(solution)/shard_map/ppermute | solution.py:50
  70.6 64.3 %collective-permute-start.11 = (bf16[4,48,1792]{2,1,0:T(8,128)(2,1)S(1)}, bf16[4,48,1792]{2,1,0:T(8,128)(2,1)S(1)}, u32[]{:S(2)}, u32[]{:S(2)}) collective-permute-start(bf16[4,48,1792]{2,1,0:T(8,128)(2,1)S(1)} %bitcast_dynamic-update-slice_fusion.12), channel_id=1, source_target_pairs={{0,8},{4,12},{8,0},{12,4},{1,9},{5,13},{9,1},{13,5},{2,10},{6,14},... | collective-permute-start | bytes 2064392 | tf_op jit(solution)/shard_map/ppermute | solution.py:50
  71.7 60.4 %collective-permute-start.10 = (bf16[4,48,1792]{2,1,0:T(8,128)(2,1)S(1)}, bf16[4,48,1792]{2,1,0:T(8,128)(2,1)S(1)}, u32[]{:S(2)}, u32[]{:S(2)}) collective-permute-start(bf16[4,48,1792]{2,1,0:T(8,128)(2,1)S(1)} %bitcast_dynamic-update-slice_fusion.12), channel_id=1, source_target_pairs={{0,4},{4,0},{8,12},{12,8},{1,5},{5,1},{9,13},{13,9},{2,6},{6,2},{1... | collective-permute-start | bytes 2064392 | tf_op jit(solution)/shard_map/ppermute | solution.py:50
  132.2 17.0 %collective-permute-start.12 = (bf16[4,48,1792]{2,1,0:T(8,128)(2,1)S(1)}, bf16[4,48,1792]{2,1,0:T(8,128)(2,1)S(1)}, u32[]{:S(2)}, u32[]{:S(2)}) collective-permute-start(bf16[4,48,1792]{2,1,0:T(8,128)(2,1)S(1)} %bitcast_dynamic-update-slice_fusion.12), channel_id=1, source_target_pairs={{0,12},{4,8},{8,4},{12,0},{1,13},{5,9},{9,5},{13,1},{2,14},{6,10},... | collective-permute-start | bytes 2064392 | tf_op jit(solution)/shard_map/ppermute | solution.py:50
  212.2 15.1 %collective-permute-start.45 = (bf16[96,768]{1,0:T(8,128)(2,1)S(1)}, bf16[96,768]{1,0:T(8,128)(2,1)S(1)}, u32[]{:S(2)}, u32[]{:S(2)}) collective-permute-start(bf16[96,768]{1,0:T(8,128)(2,1)S(1)} %get-tuple-element.105), channel_id=1, source_target_pairs={{0,65},{1,64},{64,1},{65,0},{2,67},{3,66},{66,3},{67,2},{4,69},{5,... | collective-permute-start | bytes 442376 | tf_op jit(solution)/shard_map/ppermute | solution.py:46
  212.9 18.6 %collective-permute-start.44 = (bf16[96,768]{1,0:T(8,128)(2,1)S(1)}, bf16[96,768]{1,0:T(8,128)(2,1)S(1)}, u32[]{:S(2)}, u32[]{:S(2)}) collective-permute-start(bf16[96,768]{1,0:T(8,128)(2,1)S(1)} %get-tuple-element.106), channel_id=1, source_target_pairs={{0,64},{1,65},{64,0},{65,1},{2,66},{3,67},{66,2},{67,3},{4,68},{5,... | collective-permute-start | bytes 442376 | tf_op jit(solution)/shard_map/ppermute | solution.py:46
  214.1 17.3 %collective-permute-start.43 = (bf16[96,768]{1,0:T(8,128)(2,1)S(1)}, bf16[96,768]{1,0:T(8,128)(2,1)S(1)}, u32[]{:S(2)}, u32[]{:S(2)}) collective-permute-start(bf16[96,768]{1,0:T(8,128)(2,1)S(1)} %get-tuple-element.107), channel_id=1, source_target_pairs={{0,1},{1,0},{64,65},{65,64},{2,3},{3,2},{66,67},{67,66},{4,5},{5,4... | collective-permute-start | bytes 442376 | tf_op jit(solution)/shard_map/ppermute | solution.py:46
  330.5 16.3 %collective-permute-start.61 = (bf16[4,48,768]{2,1,0:T(8,128)(2,1)S(1)}, bf16[4,48,768]{2,1,0:T(8,128)(2,1)S(1)}, u32[]{:S(2)}, u32[]{:S(2)}) collective-permute-start(bf16[4,48,768]{2,1,0:T(8,128)(2,1)S(1)} %get-tuple-element.85), channel_id=1, source_target_pairs={{0,16},{16,0},{32,48},{48,32},{1,17},{17,1},{33,49},{49,33},{2,18}... | collective-permute-start | bytes 884744 | tf_op jit(solution)/shard_map/ppermute | solution.py:50
  331.7 17.5 %collective-permute-start.63 = (bf16[4,48,768]{2,1,0:T(8,128)(2,1)S(1)}, bf16[4,48,768]{2,1,0:T(8,128)(2,1)S(1)}, u32[]{:S(2)}, u32[]{:S(2)}) collective-permute-start(bf16[4,48,768]{2,1,0:T(8,128)(2,1)S(1)} %get-tuple-element.86), channel_id=1, source_target_pairs={{0,48},{16,32},{32,16},{48,0},{1,49},{17,33},{33,17},{49,1},{2,50}... | collective-permute-start | bytes 884744 | tf_op jit(solution)/shard_map/ppermute | solution.py:50
  333.8 26.9 %collective-permute-start.62 = (bf16[4,48,768]{2,1,0:T(8,128)(2,1)S(1)}, bf16[4,48,768]{2,1,0:T(8,128)(2,1)S(1)}, u32[]{:S(2)}, u32[]{:S(2)}) collective-permute-start(bf16[4,48,768]{2,1,0:T(8,128)(2,1)S(1)} %get-tuple-element.87), channel_id=1, source_target_pairs={{0,32},{16,48},{32,0},{48,16},{1,33},{17,49},{33,1},{49,17},{2,34}... | collective-permute-start | bytes 884744 | tf_op jit(solution)/shard_map/ppermute | solution.py:50
  335.7 37.5 %collective-permute-start.58 = (bf16[256,768]{1,0:T(8,128)(2,1)S(1)}, bf16[256,768]{1,0:T(8,128)(2,1)S(1)}, u32[]{:S(2)}, u32[]{:S(2)}) collective-permute-start(bf16[256,768]{1,0:T(8,128)(2,1)S(1)} %fusion.55), channel_id=1, source_target_pairs={{0,2},{2,0},{1,3},{3,1},{4,6},{6,4},{5,7},{7,5},{8,10},{10,8},{9,1... | collective-permute-start | bytes 1179656 | tf_op jit(solution)/shard_map/ppermute | solution.py:42
  376.1 21.5 %collective-permute-start.69 = (bf16[4,48,1024]{2,1,0:T(8,128)(2,1)S(1)}, bf16[4,48,1024]{2,1,0:T(8,128)(2,1)S(1)}, u32[]{:S(2)}, u32[]{:S(2)}) collective-permute-start(bf16[4,48,1024]{2,1,0:T(8,128)(2,1)S(1)} %get-tuple-element.81), channel_id=1, source_target_pairs={{0,12},{4,8},{8,4},{12,0},{1,13},{5,9},{9,5},{13,1},{2,14},{6,10},... | collective-permute-start | bytes 1179656 | tf_op jit(solution)/shard_map/ppermute | solution.py:50
  376.8 20.9 %collective-permute-start.68 = (bf16[4,48,1024]{2,1,0:T(8,128)(2,1)S(1)}, bf16[4,48,1024]{2,1,0:T(8,128)(2,1)S(1)}, u32[]{:S(2)}, u32[]{:S(2)}) collective-permute-start(bf16[4,48,1024]{2,1,0:T(8,128)(2,1)S(1)} %get-tuple-element.82), channel_id=1, source_target_pairs={{0,8},{4,12},{8,0},{12,4},{1,9},{5,13},{9,1},{13,5},{2,10},{6,14},... | collective-permute-start | bytes 1179656 | tf_op jit(solution)/shard_map/ppermute | solution.py:50
  402.2 18.2 %collective-permute-start.59 = (bf16[128,768]{1,0:T(8,128)(2,1)S(1)}, bf16[128,768]{1,0:T(8,128)(2,1)S(1)}, u32[]{:S(2)}, u32[]{:S(2)}) collective-permute-start(bf16[128,768]{1,0:T(8,128)(2,1)S(1)} %get-tuple-element.67), channel_id=1, source_target_pairs={{0,0},{1,2},{2,1},{3,3},{64,64},{65,66},{66,65},{67,67},{4,4},{5,6... | collective-permute-start | bytes 589832 | tf_op jit(solution)/shard_map/ppermute | solution.py:38
  402.8 17.5 %collective-permute-start.60 = (bf16[128,768]{1,0:T(8,128)(2,1)S(1)}, bf16[128,768]{1,0:T(8,128)(2,1)S(1)}, u32[]{:S(2)}, u32[]{:S(2)}) collective-permute-start(bf16[128,768]{1,0:T(8,128)(2,1)S(1)} %broadcast_select_fusion.6), channel_id=1, source_target_pairs={{0,64},{1,66},{2,65},{3,67},{64,0},{65,2},{66,1},{67,3},{4,68},{5,... | collective-permute-start | bytes 589832 | tf_op jit(solution)/shard_map/ppermute | solution.py:38
  414.4 15.0 %collective-permute-start.74 = (bf16[24,4864]{1,0:T(8,128)(2,1)S(1)}, bf16[24,4864]{1,0:T(8,128)(2,1)S(1)}, u32[]{:S(2)}, u32[]{:S(2)}) collective-permute-start(bf16[24,4864]{1,0:T(8,128)(2,1)S(1)} %get-tuple-element.135), channel_id=1, source_target_pairs={{0,2},{1,0},{2,3},{3,1},{64,66},{65,64},{66,67},{67,65},{4,6},{5,4... | collective-permute-start | bytes 700424 | tf_op jit(solution)/shard_map/ppermute | solution.py:38
  (179 other events, 1613.7 us)
Sparse Core Ops, SparseCore 0:
  21.3 114.1 all-gather.1
  299.6 111.8 reduce-scatter.1
